TPU v7x, 256 devices: a whole 4x4x8 slice. The times are simulated.
256 devices in a mesh: seg: 32 (over x_hi, z, core), rad: 8 (over x_lo, y).
Axes of the slice: x: 4 (x_hi: 2, x_lo: 2; x = x_hi * 2 + x_lo), y: 4, z: 8, core: 2. Of those that a mesh axis runs over, the one named last changes fastest.
Arguments:
- start_vector: float32 [32, 3, 8, 384, 768], P('seg', None, 'rad'), may hold values from -12 to 12
- coupling: bfloat16 [32, 3, 3, 8, 384, 768], P('seg', None, None, 'rad'), may hold values from -1.796875 to 1.796875
- advect: float32 [8], P('rad'), may hold values from 0.001 to 0.004
Outputs:
- next_basis: float32 [32, 3, 8, 384, 768], P('seg', None, 'rad')
- hessenberg: float32 [6], replicated
All inputs are finite; a program needn't handle non-finite values.
Results may differ from a plain program's by a relative error of at most 0.008.
Values may be sent and summed in bfloat16 or wider, within the bound.
A program may use at most 128 MiB of HBM per device.

v0:
```python
import math

import jax
import jax.numpy as jnp
from jax import lax
from jax.sharding import PartitionSpec as P

RADIAL_ALL = 256
WINDOW_START = 124


RADIAL_GAIN = 0.25
VISC_AXIAL = 4.0
VISC_TURN = 0.05


def with_halo(block, sides, width):
    for axis, dim in sides:
        count = lax.axis_size(axis)
        forward = [(i, i + 1) for i in range(count - 1)]
        backward = [(target, source) for source, target in forward]
        low = lax.ppermute(
            lax.slice_in_dim(block, block.shape[dim] - width, None, axis=dim), axis, forward
        )
        high = lax.ppermute(lax.slice_in_dim(block, 0, width, axis=dim), axis, backward)
        block = jnp.concatenate([low, block, high], axis=dim)
    return block


def shifted(value, axis, steps):
    count = lax.axis_size(axis)
    pairs = [(source, (source + steps) % count) for source in range(count)]
    return lax.ppermute(value, axis, pairs)


def make_tables(count):
    index = jnp.arange(count, dtype=jnp.int32)
    half_len = count // 2
    freq = jnp.where(index <= half_len, index, index - half_len)
    phase = freq[:, None] * index[None, :] % count
    angle = 2.0 * math.pi / count * phase.astype(jnp.float32)
    synth = jnp.where((index <= half_len)[:, None], jnp.cos(angle), jnp.sin(angle))
    weight = jnp.where((index == 0) | (index == half_len), 1.0 / count, 2.0 / count).astype(
        jnp.float32
    )
    analysis = weight[:, None] * synth
    return (synth.astype(jnp.bfloat16), analysis.astype(jnp.bfloat16), freq)


def make_divisor(radius_index, all_rows, freq_m, freq_k, modes_m, modes_k):
    radius = (radius_index.astype(jnp.float32) + 0.5) / all_rows
    axial = (freq_k.astype(jnp.float32) / (modes_k // 2)) ** 2
    turning = (freq_m.astype(jnp.float32) / (modes_m // 2)) ** 2
    return (
        1.0
        + VISC_AXIAL * axial[None, None, :]
        + VISC_TURN * turning[None, :, None] / (radius * radius)[:, None, None]
    )


def axial_derivative(field):
    half_len = field.shape[-1] // 2
    wavenum = jnp.arange(1, half_len, dtype=jnp.int32).astype(jnp.float32)
    zeros_col = jnp.zeros(field.shape[:-1] + (1,), jnp.float32)
    return jnp.concatenate(
        [
            zeros_col,
            wavenum * field[..., half_len + 1 :],
            zeros_col,
            -wavenum * field[..., 1:half_len],
        ],
        axis=-1,
    )


def tangent(field, couple, advect, tables, divisor):
    synth_m, anal_m, synth_k, anal_k = tables
    rounded = field.astype(jnp.bfloat16)
    padded = with_halo(rounded, (("rad", 1),), 1)
    section_one = jnp.einsum(
        "crmk,kz->crmz", rounded, synth_k, preferred_element_type=jnp.float32
    ).astype(jnp.bfloat16)
    physical = jnp.einsum("mt,crmz->crtz", synth_m, section_one, preferred_element_type=jnp.float32)
    mixed = jnp.sum(couple.astype(jnp.float32) * physical[None], axis=1).astype(jnp.bfloat16)
    section_two = jnp.einsum(
        "crtz,kz->crtk", mixed, anal_k, preferred_element_type=jnp.float32
    ).astype(jnp.bfloat16)
    spectral = jnp.einsum("mt,crtk->crmk", anal_m, section_two, preferred_element_type=jnp.float32)
    deriv = axial_derivative(field)
    widened = padded.astype(jnp.float32)
    radial = RADIAL_GAIN * (widened[:, 2:] - 2.0 * widened[:, 1:-1] + widened[:, :-2])
    return (field + spectral - advect[None, :, None, None] * deriv + radial) / divisor


def apply(vector, couple, advect, tables, divisor, received):
    field = vector
    field = tangent(field, couple, advect, tables, divisor)
    received = shifted(vector.astype(jnp.bfloat16), "seg", -1).astype(vector.dtype)
    return (field - received, received)


def projected(values, cells):
    return lax.psum(jnp.stack(values) / cells, ("seg", "rad"))


def length_sum(value, cells):
    return lax.psum(value / cells, ("seg", "rad"))


def on_device(start_vector, coupling, advect):
    vector = start_vector[0]
    couple = coupling[0]
    chans, rows_here, modes_m, modes_k = vector.shape
    all_rows = rows_here * lax.axis_size("rad")
    cells = float(lax.axis_size("seg") * chans * all_rows * modes_m * modes_k)
    synth_m, anal_m, freq_m = make_tables(modes_m)
    synth_k, anal_k, freq_k = make_tables(modes_k)
    tables = (synth_m, anal_m, synth_k, anal_k)
    radius_index = (
        WINDOW_START + lax.axis_index("rad") * rows_here + jnp.arange(rows_here, dtype=jnp.int32)
    )
    divisor = make_divisor(radius_index, RADIAL_ALL, freq_m, freq_k, modes_m, modes_k)
    total = lax.psum(jnp.sum(vector * vector) / cells, ("seg", "rad"))
    start_norm = jnp.sqrt(total)
    basis_one = vector / start_norm
    image_one, shifted_one = apply(basis_one, couple, advect, tables, divisor, None)
    upper_one = projected([jnp.sum(image_one * basis_one)], cells)[0]
    residual_one = image_one - upper_one * basis_one
    lower_one = jnp.sqrt(length_sum(jnp.sum(residual_one * residual_one), cells))
    basis_two = residual_one / lower_one
    image_two, unused = apply(basis_two, couple, advect, tables, divisor, None)
    sums_two = projected([jnp.sum(image_two * basis_one), jnp.sum(image_two * basis_two)], cells)
    upper_two = sums_two[0]
    middle_two = sums_two[1]
    residual_two = image_two - upper_two * basis_one - middle_two * basis_two
    lower_two = jnp.sqrt(length_sum(jnp.sum(residual_two * residual_two), cells))
    next_basis = residual_two / lower_two
    hessenberg = jnp.stack([start_norm, upper_one, lower_one, upper_two, middle_two, lower_two])
    return (next_basis[None], hessenberg)


def solution(mesh):
    return jax.shard_map(
        on_device,
        mesh=mesh,
        in_specs=(
            P("seg", None, "rad", None, None),
            P("seg", None, None, "rad", None, None),
            P("rad"),
        ),
        out_specs=(P("seg", None, "rad", None, None), P()),
        check_vma=False,
    )
```

profile of v0, /device:TPU:1, one launch (start us, length us, event | category | flops | bytes accessed | tf_op | source)
XLA Modules:
  0.0 573.7 jit_solution(4091980021766297315)
XLA Ops:
  0.6 0.0 copy-start.1
  0.6 3.7 multiply_reduce_fusion.5
  5.0 0.0 copy-done.1
  5.0 2.9 copy.5
  7.9 81.3 %psum.35 = f32[]{:T(128)} all-reduce(f32[]{:T(128)S(6)} %div.96), channel_id=1, replica_groups=mesh['seg'=32,'rad'=8] {'seg','rad'}, use_global_device_ids=true, to_apply=%region_1.2 | all-reduce | flops 1 | bytes 8 | tf_op jit(solution)/shard_map/psum | solution.py:123
  89.9 3.7 fusion.146
  93.6 2.5 collective-permute-start
  96.1 1.3 collective-permute-start.1
  97.4 1.2 collective-permute-start.2
  98.6 0.5 iota_compare_fusion.2
  99.1 0.5 iota_compare_fusion.5
  99.7 0.6 fusion.108
  100.3 0.6 fusion.110
  100.9 14.6 %fusion.202 = bf16[3,384,768]{1,2,0:T(8,128)(2,1)} fusion(f32[1,3,1,384,768]{3,4,1,2,0:T(8,128)} %copy.5, f32[]{:T(128)} %sqrt.9, s32[768]{0:T(1024)S(1)} %add_select_fusion.2, pred[768]{0:T(1024)(128)(4,1)} %iota_compare_fusion.2), kind=kOutput, calls=%fused_computation.69.clone.2 | convolution fusion | flops 1368096768 | bytes 5312260 | tf_op jit(solution)/shard_map/crmk,kz->crmz/dot_general | solution.py:80
  115.4 7.3 %convolution_bitcast_fusion.1 = f32[3,384,768]{1,2,0:T(8,128)} fusion(s32[384]{0:T(512)S(1)} %add_select_fusion.3, pred[384]{0:T(512)(128)(4,1)} %iota_compare_fusion.5, bf16[3,384,768]{1,2,0:T(8,128)(2,1)} %fusion.202), kind=kOutput, calls=%fused_computation.51 | convolution fusion | flops 681099264 | bytes 5310336 | tf_op jit(solution)/shard_map/mt,crmz->crtz/dot_general | solution.py:83
  122.8 5.2 copy.6
  128.6 0.2 broadcast_add_fusion
  128.8 0.4 slice_multiply_fusion.5
  129.2 2.0 copy-done.2
  131.2 3.7 fusion
  134.9 0.0 copy-done.9
  134.9 0.0 copy-done.11
  134.9 0.0 copy-done.15
  134.9 13.6 %fusion.32.clone.5 = bf16[3,384,768]{1,2,0:T(8,128)(2,1)S(1)} fusion(bf16[3,384,768]{2,1,0:T(8,128)(2,1)S(1)} %fusion, f32[768]{0:T(1024)S(1)} %copy-done.11, s32[768]{0:T(1024)S(1)} %copy-done.9, pred[768]{0:T(1024)(128)(4,1)S(1)} %copy-done.15), kind=kOutput, calls=%fused_computation.66.clone.clone.clone.2 | convolution fusion | flops 1366917120 | bytes 3545856 | tf_op jit(solution)/shard_map/crtz,kz->crtk/dot_general | solution.py:85
  148.5 0.0 copy-start.7
  148.5 0.0 copy-start.13
  148.5 0.0 collective-permute-done
  148.5 0.0 collective-permute-done.1
  148.5 3.4 maximum_convert_fusion
  151.9 0.0 collective-permute-done.2
  151.9 0.0 copy-done.4
  151.9 0.0 copy-done.7
  152.0 0.0 copy-done.13
  152.0 0.0 copy-start.6
  152.0 8.8 %multiply_reduce_fusion.4 = (f32[]{:T(128)}, f32[3,1,384,768]{2,3,0,1:T(8,128)}) fusion(f32[3,1,384,768]{2,3,0,1:T(8,128)S(1)} %get-tuple-element.12, bf16[3,1,384,768]{2,3,0,1:T(8,128)(2,1)} %collective-permute-done.2, f32[384,768]{0,1:T(8,128)S(1)} %broadcast_add_fusion, f32[3,3,384,768]{2,3,0,1:T(8,128)S(1)} %maximum_convert_fusion, ...), kind=kOutput, calls=%fused_computation.39 | convolution fusion | flops 695402496 | bytes 25951112 | tf_op jit(solution)/shard_map/mt,crtk->crmk/dot_general | solution.py:88
  161.5 83.7 %psum.36 = f32[1]{0:T(128)} all-reduce(f32[1]{0:T(128)} %bitcast.13), channel_id=1, replica_groups=mesh['seg'=32,'rad'=8] {'seg','rad'}, use_global_device_ids=true, to_apply=%region_4.5 | all-reduce | flops 1 | bytes 8 | tf_op jit(solution)/shard_map/psum | solution.py:103
  245.1 4.2 multiply_reduce_fusion.3
  250.1 4.1 fusion.198
  254.2 72.7 %psum.37 = f32[]{:T(128)} all-reduce(f32[]{:T(128)S(6)} %div.108), channel_id=1, replica_groups=mesh['seg'=32,'rad'=8] {'seg','rad'}, use_global_device_ids=true, to_apply=%region_6.7 | all-reduce | flops 1 | bytes 8 | tf_op jit(solution)/shard_map/psum | solution.py:107
  327.7 5.5 fusion.145
  333.2 3.8 collective-permute-start.3
  337.0 1.3 collective-permute-start.4
  338.3 1.1 collective-permute-start.5
  339.3 15.7 %convolution_bitcast_fusion = f32[3,384,768]{1,2,0:T(8,128)} fusion(bf16[3,1,384,768]{2,3,0,1:T(8,128)(2,1)} %get-tuple-element.9, s32[768]{0:T(1024)} %copy-done.8, pred[768]{0:T(1024)(128)(4,1)} %iota_compare_fusion.2, bf16[384,384,1]{1,0,2:T(8,128)(2,1)} %fusion.198), kind=kOutput, calls=%fused_computation.50 | convolution fusion | flops 2045804544 | bytes 5607168 | tf_op jit(solution)/shard_map/mt,crmz->crtz/dot_general | solution.py:83
  355.0 5.2 copy.7
  360.2 3.7 slice_multiply_fusion.3
  363.9 3.7 fusion.1
  367.6 13.6 %fusion.206 = bf16[3,384,768]{1,2,0:T(8,128)(2,1)S(1)} fusion(bf16[3,384,768]{2,1,0:T(8,128)(2,1)S(1)} %fusion.1, f32[768]{0:T(1024)S(1)} %copy-done.12, s32[768]{0:T(1024)S(1)} %copy-done.10, pred[768]{0:T(1024)(128)(4,1)S(1)} %copy-done.16), kind=kOutput, calls=%fused_computation.61.clone.2 | convolution fusion | flops 1366917120 | bytes 3545856 | tf_op jit(solution)/shard_map/crtz,kz->crtk/dot_general | solution.py:85
  381.3 3.6 fusion.27
  384.9 0.0 collective-permute-done.3
  384.9 0.0 collective-permute-done.4
  384.9 0.0 copy-start
  384.9 3.5 maximum_convert_fusion.1
  388.4 0.0 collective-permute-done.5
  388.5 0.4 copy-done
  388.8 6.3 %multiply_reduce_fusion.2 = (f32[]{:T(128)}, f32[]{:T(128)}, f32[3,1,384,768]{2,3,0,1:T(8,128)}) fusion(f32[3,1,384,768]{2,3,0,1:T(8,128)S(1)} %get-tuple-element.12, f32[3,1,384,768]{2,3,0,1:T(8,128)S(1)} %copy-done, bf16[3,1,384,768]{2,3,0,1:T(8,128)(2,1)} %collective-permute-done.5, f32[384,768]{0,1:T(8,128)S(1)} %copy-done.5, ...), kind=kLoop, calls=%fused_computation.36 | loop fusion | flops 15925246 | bytes 31256076 | tf_op jit(solution)/shard_map/reduce_sum | solution.py:132
  395.2 1.4 maximum_multiply_fusion
  396.5 88.5 %psum.38 = f32[2]{0:T(128)S(1)} all-reduce(f32[2]{0:T(128)S(1)} %maximum_multiply_fusion), channel_id=1, replica_groups=mesh['seg'=32,'rad'=8] {'seg','rad'}, use_global_device_ids=true, to_apply=%region_10.11 | all-reduce | flops 2 | bytes 16 | tf_op jit(solution)/shard_map/psum | solution.py:103
  485.1 0.6 fusion.148
  485.6 7.5 %multiply_reduce_fusion = (f32[]{:T(128)}, f32[3,1,384,768]{2,3,0,1:T(8,128)}) fusion(f32[3,1,384,768]{2,3,0,1:T(8,128)} %get-tuple-element.10, f32[]{:T(128)} %bitcast.25, f32[3,1,384,768]{2,3,0,1:T(8,128)} %get-tuple-element.8, f32[3,1,384,768]{2,3,0,1:T(8,128)S(1)} %get-tuple-element.12, f32[]{:T(128)} %bitcast.24), kind=kLoop, calls=%fused_computation.33 | loop fusion | flops 5308415 | bytes 14155788 | tf_op jit(solution)/shard_map/reduce_sum | solution.py:136
  493.7 72.6 %psum.39 = f32[]{:T(128)} all-reduce(f32[]{:T(128)S(6)} %div.113), channel_id=1, replica_groups=mesh['seg'=32,'rad'=8] {'seg','rad'}, use_global_device_ids=true, to_apply=%region_12.13 | all-reduce | flops 1 | bytes 8 | tf_op jit(solution)/shard_map/psum | solution.py:107
  567.0 2.2 divide_bitcast_fusion
  569.3 2.9 copy.8
  572.2 1.2 stack.29
  (27 shorter events, 0.1 us)
Async XLA Ops:
  0.6 4.3 copy-start.1
  93.6 55.0 %collective-permute-start = (bf16[3,1,384,768]{2,3,0,1:T(8,128)(2,1)}, bf16[3,1,384,768]{2,3,0,1:T(8,128)(2,1)}, u32[]{:S(2)}, u32[]{:S(2)}) collective-permute-start(bf16[3,1,384,768]{2,3,0,1:T(8,128)(2,1)} %get-tuple-element.11), channel_id=1, source_target_pairs={{0,1},{1,2},{2,3},{3,4},{4,5},{5,6},{6,7},{8,9},{9,10},{10,11},{11... | collective-permute-start | bytes 5308424 | tf_op jit(solution)/shard_map/ppermute | solution.py:22
  96.1 52.4 %collective-permute-start.1 = (bf16[3,1,384,768]{2,3,0,1:T(8,128)(2,1)}, bf16[3,1,384,768]{2,3,0,1:T(8,128)(2,1)}, u32[]{:S(2)}, u32[]{:S(2)}) collective-permute-start(bf16[3,1,384,768]{2,3,0,1:T(8,128)(2,1)} %get-tuple-element.11), channel_id=1, source_target_pairs={{1,0},{2,1},{3,2},{4,3},{5,4},{6,5},{7,6},{9,8},{10,9},{11,10},{12... | collective-permute-start | bytes 5308424 | tf_op jit(solution)/shard_map/ppermute | solution.py:25
  97.4 54.5 %collective-permute-start.2 = (bf16[3,1,384,768]{2,3,0,1:T(8,128)(2,1)}, bf16[3,1,384,768]{2,3,0,1:T(8,128)(2,1)}, u32[]{:S(2)}, u32[]{:S(2)}) collective-permute-start(bf16[3,1,384,768]{2,3,0,1:T(8,128)(2,1)} %get-tuple-element.11), channel_id=1, source_target_pairs={{0,248},{8,0},{16,8},{24,16},{32,24},{40,32},{48,40},{56,48},{64,5... | collective-permute-start | bytes 5308424 | tf_op jit(solution)/shard_map/ppermute | solution.py:33
  98.6 16.8 %copy-start.8 = (s32[768]{0:T(1024)}, s32[768]{0:T(1024)S(1)}, u32[]{:S(2)}) copy-start(s32[768]{0:T(1024)S(1)} %add_select_fusion.2) | copy-start | bytes 9220
  128.8 23.2 %copy-start.4 = (f32[384,768]{0,1:T(8,128)}, f32[384,768]{0,1:T(8,128)S(1)}, u32[]{:S(2)}) copy-start(f32[384,768]{0,1:T(8,128)S(1)} %broadcast_add_fusion) | copy-start | bytes 3538948
  128.8 2.4 copy-start.2
  131.2 3.7 copy-start.9
  131.2 3.7 copy-start.11
  131.2 3.7 copy-start.15
  148.5 3.4 copy-start.7
  148.5 3.4 copy-start.13
  152.0 8.9 %copy-start.6 = (f32[3,1,384,1]{2,3,0,1:T(1,128)}, f32[3,1,384,1]{2,3,0,1:T(1,128)S(1)}, u32[]{:S(2)}) copy-start(f32[3,1,384,1]{2,3,0,1:T(1,128)S(1)} %concatenate.30) | copy-start | bytes 13828
  333.2 51.7 %collective-permute-start.3 = (bf16[3,1,384,768]{2,3,0,1:T(8,128)(2,1)}, bf16[3,1,384,768]{2,3,0,1:T(8,128)(2,1)}, u32[]{:S(2)}, u32[]{:S(2)}) collective-permute-start(bf16[3,1,384,768]{2,3,0,1:T(8,128)(2,1)} %get-tuple-element.9), channel_id=1, source_target_pairs={{0,1},{1,2},{2,3},{3,4},{4,5},{5,6},{6,7},{8,9},{9,10},{10,11},{11... | collective-permute-start | bytes 5308424 | tf_op jit(solution)/shard_map/ppermute | solution.py:22
  337.0 47.9 %collective-permute-start.4 = (bf16[3,1,384,768]{2,3,0,1:T(8,128)(2,1)}, bf16[3,1,384,768]{2,3,0,1:T(8,128)(2,1)}, u32[]{:S(2)}, u32[]{:S(2)}) collective-permute-start(bf16[3,1,384,768]{2,3,0,1:T(8,128)(2,1)} %get-tuple-element.9), channel_id=1, source_target_pairs={{1,0},{2,1},{3,2},{4,3},{5,4},{6,5},{7,6},{9,8},{10,9},{11,10},{12... | collective-permute-start | bytes 5308424 | tf_op jit(solution)/shard_map/ppermute | solution.py:25
  338.3 50.2 %collective-permute-start.5 = (bf16[3,1,384,768]{2,3,0,1:T(8,128)(2,1)}, bf16[3,1,384,768]{2,3,0,1:T(8,128)(2,1)}, u32[]{:S(2)}, u32[]{:S(2)}) collective-permute-start(bf16[3,1,384,768]{2,3,0,1:T(8,128)(2,1)} %get-tuple-element.9), channel_id=1, source_target_pairs={{0,248},{8,0},{16,8},{24,16},{32,24},{40,32},{48,40},{56,48},{64,5... | collective-permute-start | bytes 5308424 | tf_op jit(solution)/shard_map/ppermute | solution.py:33
  360.2 3.7 copy-start.3
  363.9 3.7 copy-start.10
  363.9 3.7 copy-start.12
  363.9 3.7 copy-start.16
  367.6 13.6 %copy-start.14 = (pred[384]{0:T(512)(128)(4,1)S(1)}, pred[384]{0:T(512)(128)(4,1)}, u32[]{:S(2)}) copy-start(pred[384]{0:T(512)(128)(4,1)} %iota_compare_fusion.5) | copy-start | bytes 1156
  384.9 3.6 copy-start.5
  384.9 3.9 copy-start
where the time goes:
time: 578 us; the launch traced here: 574 us
  blocking collectives  399 us (69%)
  matrix products  77.2 us (13%)
  other arithmetic  59.5 us (10%)
  local copies, waits for them, and re-layouts  20.5 us (4%)
  starting transfers between devices  11.1 us (2%)
  between operations  6.56 us (1%)
    psum x2, blocking collectives, projected(): return lax.psum(jnp.stack(values) / cells, ('seg', 'rad'))  172 us
    psum x2, blocking collectives, length_sum(): return lax.psum(value / cells, ('seg', 'rad'))  145 us
    psum x1, blocking collectives, on_device(): total = lax.psum(jnp.sum(vector * vector) / cells, ('seg', 'rad'))  81.3 us
    dot_general x2, matrix products, tangent(): jnp.einsum('crtz,kz->crtk', mixed, anal_k, preferred_element_type=jnp.flo...  27.2 us
    dot_general x2, matrix products, tangent(): jnp.einsum('mt,crmz->crtz', synth_m, section_one, preferred_element_type=...  23 us
    dot_general x1, matrix products, tangent(): jnp.einsum('crmk,kz->crmz', rounded, synth_k, preferred_element_type=jnp....  14.6 us
    dot_general x2, matrix products, tangent(): jnp.einsum('mt,crtk->crmk', anal_m, section_two, preferred_element_type=j...  12.4 us
  transfers between devices with their start and end apart: 6, of which 0 were waited for; matrix products, arithmetic and copies ran while one was open for 17% of the time, Pallas kernels for 0%

commit v1 on v0

v1 whole, which is shorter than its diff:
```python
import functools
import math

import jax
import jax.numpy as jnp
import numpy as np
from jax import lax
from jax.experimental import pallas as pl
from jax.experimental.pallas import tpu as pltpu
from jax.sharding import PartitionSpec as P

RADIAL_ALL = 256
WINDOW_START = 124
RADIAL_GAIN = 0.25
VISC_AXIAL = 4.0
VISC_TURN = 0.05

MESH = pl.DeviceIdType.MESH
F32 = jnp.float32
BF16 = jnp.bfloat16
PARTS = 2
STRIP = 16
TILE = 256


def make_tables(count):
    index = np.arange(count)
    half = count // 2
    freq = np.where(index <= half, index, index - half)
    angle = 2.0 * np.pi / count * (freq[:, None] * index[None, :] % count)
    synth = np.where((index <= half)[:, None], np.cos(angle), np.sin(angle))
    weight = np.where((index == 0) | (index == half), 1.0 / count, 2.0 / count)
    analysis = weight[:, None] * synth
    as_bf16 = lambda table: jnp.asarray(table.astype(np.float32).astype(jnp.bfloat16))
    return as_bf16(synth), as_bf16(analysis)


def fold(value):
    total = None
    for row in range(0, value.shape[0], 8):
        for lane in range(0, value.shape[1], 128):
            piece = value[row : row + 8, lane : lane + 128]
            total = piece if total is None else total + piece
    return total


def dot(left, right):
    return jnp.dot(left, right, preferred_element_type=F32)


def steps_kernel(
    sizes, cells,
    v_hbm, couple_hbm, advect_ref, synth_k_hbm, anal_k_hbm, synth_m_hbm, anal_m_hbm,
    w1_hbm, w2_hbm, coef_ref,
    v_buf, couple, synth_k, anal_k, synth_m, anal_m,
    sent_a, sent_b, low_a, high_a, next_a, low_b, high_b, next_b,
    w1_buf, spec, mixed, inv_div, grams, slots_one, slots_two,
    load_sem, v_sem, out_sem,
    send_sem, recv_sem, sum_send, sum_recv,
):
    segs, rads, group = sizes
    chans, modes_m, modes_k = v_buf.shape
    rows = modes_m // PARTS
    pieces = [(c, q) for c in range(chans) for q in range(PARTS)]
    seg = lax.axis_index("seg")
    rad = lax.axis_index("rad")
    seg_prev = lax.rem(seg + segs - 1, segs)
    seg_next = lax.rem(seg + 1, segs)
    base = (seg // group) * group
    one_me = seg - base
    spread = segs // group
    two_count = spread * rads
    two_me = (seg // group) * rads + rad

    def one_peer(d):
        return lax.rem(one_me + d, group)

    def two_peer(d):
        other = lax.rem(two_me + d, two_count)
        return other, ((other // rads) * group + one_me, lax.rem(other, rads))

    loads = [
        pltpu.make_async_copy(source, target, load_sem.at[i])
        for i, (source, target) in enumerate(
            [
                (synth_k_hbm, synth_k),
                (synth_m_hbm, synth_m),
                (couple_hbm, couple),
                (anal_k_hbm, anal_k),
                (anal_m_hbm, anal_m),
            ]
        )
    ]
    v_loads = []
    for i, (c, q) in enumerate(pieces):
        at = (c, pl.ds(q * rows, rows))
        v_loads.append(pltpu.make_async_copy(v_hbm.at[at], v_buf.at[at], v_sem.at[i]))
        v_loads[-1].start()
    for load in loads:
        load.start()

    barrier = pltpu.get_barrier_semaphore()
    for d in range(1, group):
        pl.semaphore_signal(barrier, inc=1, device_id=(base + one_peer(d), rad), device_id_type=MESH)
    for d in range(1, two_count):
        pl.semaphore_signal(barrier, inc=1, device_id=two_peer(d)[1], device_id_type=MESH)
    for other in (seg_prev, seg_next):
        pl.semaphore_signal(barrier, inc=1, device_id=(other, rad), device_id_type=MESH)

    @pl.when(rad == 0)
    def _():
        low_a[...] = jnp.zeros_like(low_a)
        low_b[...] = jnp.zeros_like(low_b)

    @pl.when(rad == rads - 1)
    def _():
        high_a[...] = jnp.zeros_like(high_a)
        high_b[...] = jnp.zeros_like(high_b)

    def sends(phase, i):
        c, q = pieces[i]
        at = (c, pl.ds(q * rows, rows))
        source = (sent_a, sent_b)[phase]
        low, high, nxt = ((low_a, high_a, next_a), (low_b, high_b, next_b))[phase]

        def copy(way, target, device):
            return pltpu.make_async_remote_copy(
                src_ref=source.at[at], dst_ref=target.at[at],
                send_sem=send_sem.at[phase, way, i], recv_sem=recv_sem.at[phase, way, i],
                device_id=device, device_id_type=MESH,
            )

        return (
            copy(0, low, (seg, lax.rem(rad + 1, rads))),
            copy(1, high, (seg, lax.rem(rad + rads - 1, rads))),
            copy(2, nxt, (seg_prev, rad)),
        )

    def start_sends(phase, i):
        up, down, back = sends(phase, i)

        @pl.when(rad < rads - 1)
        def _():
            up.start()

        @pl.when(rad > 0)
        def _():
            down.start()

        back.start()

    def wait_recvs(phase, i):
        up, down, back = sends(phase, i)

        @pl.when(rad > 0)
        def _():
            up.wait_recv()

        @pl.when(rad < rads - 1)
        def _():
            down.wait_recv()

        back.wait_recv()

    def wait_sends(phase, i):
        up, down, back = sends(phase, i)

        @pl.when(rad < rads - 1)
        def _():
            up.wait_send()

        @pl.when(rad > 0)
        def _():
            down.wait_send()

        back.wait_send()

    def strips(c, q, body, carry):
        def step(j, carry):
            row = pl.multiple_of(q * rows + j * STRIP, STRIP)
            return body(row, pl.ds(row, STRIP), carry)

        return lax.fori_loop(0, rows // STRIP, step, carry)

    zero = jnp.zeros((8, 128), F32)
    gram = [zero] * 6
    for i, (c, q) in enumerate(pieces):
        v_loads[i].wait()

        def rounding(row, at, total, c=c):
            value = v_buf[c, at, :]
            sent_a[c, at, :] = value.astype(BF16)
            return total + fold(value * value)

        gram[0] = strips(c, q, rounding, gram[0])
        if i == 0:
            pl.semaphore_wait(barrier, group - 1 + two_count - 1 + 2)
        start_sends(0, i)

    def freq(index, count):
        return jnp.where(index <= count // 2, index, index - count // 2).astype(F32)

    freq_k = freq(lax.broadcasted_iota(jnp.int32, (1, modes_k), 1), modes_k)
    axial = VISC_AXIAL * (freq_k / (modes_k // 2)) ** 2
    wavenum = freq(lax.broadcasted_iota(jnp.int32, (1, modes_k), 1), modes_k)
    column = lax.broadcasted_iota(jnp.int32, (1, modes_k), 1)
    half = modes_k // 2
    wavenum = jnp.where(column < half, column, half - column).astype(F32)
    wavenum = wavenum * advect_ref[0]
    radius = (jnp.full((1, modes_k), rad + WINDOW_START, jnp.int32).astype(F32) + 0.5) / RADIAL_ALL

    def divide(j, _):
        row = pl.multiple_of(j * STRIP, STRIP)
        freq_m = freq(row + lax.broadcasted_iota(jnp.int32, (STRIP, modes_k), 0), modes_m)
        turning = (freq_m / (modes_m // 2)) ** 2
        inv_div[pl.ds(row, STRIP), :] = 1.0 / (1.0 + axial + VISC_TURN * turning / (radius * radius))
        return 0

    lax.fori_loop(0, modes_m // STRIP, divide, 0)

    def spectral(source):
        def synthesis(j, _):
            at = pl.ds(pl.multiple_of(j * TILE, TILE), TILE)
            physical = [
                dot(synth_m[...], dot(source[c], synth_k[:, at]).astype(BF16)) for c in range(chans)
            ]
            for c in range(chans):
                total = couple[c, 0, :, at].astype(F32) * physical[0]
                for k in range(1, chans):
                    total += couple[c, k, :, at].astype(F32) * physical[k]
                mixed[c, :, at] = total.astype(BF16)
            return 0

        lax.fori_loop(0, modes_k // TILE, synthesis, 0)

        def analysis(step, _):
            c = step // (modes_k // TILE)
            j = lax.rem(step, modes_k // TILE)
            at = pl.ds(pl.multiple_of(j * TILE, TILE), TILE)
            section = dot(mixed[c], anal_k[:, at]).astype(BF16)
            spec[c, :, at] = dot(anal_m[...], section)
            return 0

        lax.fori_loop(0, chans * (modes_k // TILE), analysis, 0)

    def image(field, bufs, c, at):
        sent, low, high, nxt = bufs
        swapped = jnp.concatenate([field[:, half:], field[:, :half]], axis=1)
        outer = low[c, at, :].astype(F32) + high[c, at, :].astype(F32)
        radial = RADIAL_GAIN * (outer - 2.0 * sent[c, at, :].astype(F32))
        total = field + spec[c, at, :] - wavenum * swapped + radial
        return total * inv_div[at, :] - nxt[c, at, :].astype(F32)

    for load in loads:
        load.wait()
    spectral(sent_a)

    w1_outs = []
    for i, (c, q) in enumerate(pieces):
        wait_recvs(0, i)

        def first(row, at, totals, c=c):
            field = v_buf[c, at, :]
            value = image(field, (sent_a, low_a, high_a, next_a), c, at)
            w1_buf[c, at, :] = value
            sent_b[c, at, :] = value.astype(BF16)
            return totals[0] + fold(value * field), totals[1] + fold(value * value)

        gram[1], gram[2] = strips(c, q, first, (gram[1], gram[2]))
        start_sends(1, i)
        at = (c, pl.ds(q * rows, rows))
        w1_outs.append(pltpu.make_async_copy(w1_buf.at[at], w1_hbm.at[at], out_sem.at[0, i]))
        w1_outs[-1].start()

    spectral(sent_b)

    w2_outs = []
    for i, (c, q) in enumerate(pieces):
        wait_recvs(1, i)

        def second(row, at, totals, c=c):
            field = w1_buf[c, at, :]
            value = image(field, (sent_b, low_b, high_b, next_b), c, at)
            spec[c, at, :] = value
            return (
                totals[0] + fold(value * v_buf[c, at, :]),
                totals[1] + fold(value * field),
                totals[2] + fold(value * value),
            )

        gram[3], gram[4], gram[5] = strips(c, q, second, (gram[3], gram[4], gram[5]))
        at = (c, pl.ds(q * rows, rows))
        w2_outs.append(pltpu.make_async_copy(spec.at[at], w2_hbm.at[at], out_sem.at[1, i]))
        w2_outs[-1].start()

    mine = jnp.concatenate([jnp.sum(value, axis=0, keepdims=True) for value in gram] + [zero[:2]], axis=0)

    def add_up(stage, slots, me, count, peer):
        def copy(d, slot):
            return pltpu.make_async_remote_copy(
                src_ref=slots.at[slot], dst_ref=slots.at[slot],
                send_sem=sum_send.at[stage, d], recv_sem=sum_recv.at[stage, d],
                device_id=peer(d), device_id_type=MESH,
            )

        for d in range(1, count):
            copy(d, me).start()
        for d in range(1, count):
            copy(d, lax.rem(me + count - d, count)).wait_recv()
        total = slots[0]
        for slot in range(1, count):
            total = total + slots[slot]
        for d in range(1, count):
            copy(d, me).wait_send()
        return total

    slots_one[one_me] = mine
    partial = add_up(0, slots_one, one_me, group, lambda d: (base + one_peer(d), rad))
    slots_two[two_me] = partial
    sums = add_up(1, slots_two, two_me, two_count, lambda d: two_peer(d)[1])
    sums = jnp.broadcast_to(jnp.sum(sums, axis=1, keepdims=True), (8, 128)) * (1.0 / cells)
    g00, g01, g11, g02, g12, g22 = (sums[i : i + 1] for i in range(6))
    start_norm = jnp.sqrt(g00)
    upper_one = g01 / g00
    lower_one = jnp.sqrt(g11 / g00 - upper_one * upper_one)
    scale = start_norm * lower_one
    upper_two = (g02 - upper_one * g01) / (g00 * lower_one)
    middle_two = (g12 - upper_one * (g02 + g11) + upper_one * upper_one * g01) / (scale * scale)
    length = (g22 - 2.0 * upper_one * g12 + upper_one * upper_one * g11) / (scale * scale)
    lower_two = jnp.sqrt(length - upper_two * upper_two - middle_two * middle_two)
    on_two = 1.0 / (scale * lower_two)
    on_one = -(upper_one + middle_two) * on_two
    on_start = (middle_two * upper_one / scale - upper_two / start_norm) / lower_two
    coef_ref[0:8, :] = jnp.concatenate(
        [start_norm, upper_one, lower_one, upper_two, middle_two, lower_two, on_two, on_one], axis=0
    )
    coef_ref[8:16, :] = jnp.broadcast_to(on_start, (8, 128))

    for i in range(len(pieces)):
        wait_sends(0, i)
        wait_sends(1, i)
        w1_outs[i].wait()
        w2_outs[i].wait()


def combine_kernel(coef_ref, v_ref, w1_ref, w2_ref, out_ref, hess_ref):
    on_two = coef_ref[6:7, 0:1]
    on_one = coef_ref[7:8, 0:1]
    on_start = coef_ref[8:9, 0:1]
    out_ref[0] = on_two * w2_ref[0] + on_one * w1_ref[0] + on_start * v_ref[0]

    @pl.when(pl.program_id(0) == 0)
    def _():
        for i in range(6):
            hess_ref[i] = coef_ref[i, 0]


def on_device(segs, rads, start_vector, coupling, advect):
    shape = start_vector.shape
    chans, modes_m, modes_k = shape[1], shape[3], shape[4]
    vector = start_vector.reshape(chans, modes_m, modes_k)
    couple = coupling.reshape(chans, chans, modes_m, modes_k)
    cells = float(segs * rads * chans * modes_m * modes_k)
    synth_m, anal_m = make_tables(modes_m)
    synth_k, anal_k = make_tables(modes_k)
    group = 16
    two_count = (segs // group) * rads
    field = (chans, modes_m, modes_k)
    count = chans * PARTS
    any_space = pl.BlockSpec(memory_space=pl.ANY)
    w1, w2, coef = pl.pallas_call(
        functools.partial(steps_kernel, (segs, rads, group), cells),
        out_shape=(
            jax.ShapeDtypeStruct(field, F32),
            jax.ShapeDtypeStruct(field, F32),
            jax.ShapeDtypeStruct((16, 128), F32),
        ),
        in_specs=[any_space, any_space, pl.BlockSpec(memory_space=pltpu.SMEM)] + [any_space] * 4,
        out_specs=(any_space, any_space, pl.BlockSpec(memory_space=pltpu.VMEM)),
        scratch_shapes=[
            pltpu.VMEM(field, F32),
            pltpu.VMEM((chans,) + field, BF16),
            pltpu.VMEM((modes_k, modes_k), BF16),
            pltpu.VMEM((modes_k, modes_k), BF16),
            pltpu.VMEM((modes_m, modes_m), BF16),
            pltpu.VMEM((modes_m, modes_m), BF16),
        ]
        + [pltpu.VMEM(field, BF16)] * 8
        + [
            pltpu.VMEM(field, F32),
            pltpu.VMEM(field, F32),
            pltpu.VMEM(field, BF16),
            pltpu.VMEM((modes_m, modes_k), F32),
            pltpu.VMEM((8, 128), F32),
            pltpu.VMEM((group, 8, 128), F32),
            pltpu.VMEM((two_count, 8, 128), F32),
            pltpu.SemaphoreType.DMA((5,)),
            pltpu.SemaphoreType.DMA((count,)),
            pltpu.SemaphoreType.DMA((2, count)),
            pltpu.SemaphoreType.DMA((2, 3, count)),
            pltpu.SemaphoreType.DMA((2, 3, count)),
            pltpu.SemaphoreType.DMA((2, 16)),
            pltpu.SemaphoreType.DMA((2, 16)),
        ],
        compiler_params=pltpu.CompilerParams(
            collective_id=0, has_side_effects=True, vmem_limit_bytes=50 * 1024 * 1024
        ),
    )(vector, couple, advect, synth_k, anal_k.T, synth_m.T, anal_m)
    block = (1, modes_m // 2, modes_k)
    block_spec = pl.BlockSpec(block, lambda c, q: (c, q, 0))
    out, hess = pl.pallas_call(
        combine_kernel,
        grid=(chans, 2),
        out_shape=(jax.ShapeDtypeStruct(field, F32), jax.ShapeDtypeStruct((6,), F32)),
        in_specs=[pl.BlockSpec((16, 128), lambda c, q: (0, 0))] + [block_spec] * 3,
        out_specs=(block_spec, pl.BlockSpec(memory_space=pltpu.SMEM)),
    )(coef, vector, w1, w2)
    return out.reshape(shape), hess


def solution(mesh):
    return jax.shard_map(
        functools.partial(on_device, mesh.shape["seg"], mesh.shape["rad"]),
        mesh=mesh,
        in_specs=(
            P("seg", None, "rad", None, None),
            P("seg", None, None, "rad", None, None),
            P("rad"),
        ),
        out_specs=(P("seg", None, "rad", None, None), P()),
        check_vma=False,
    )
```

time: 578 us -> 152 us (0.26)
  blocking collectives: 399 us -> 0 us
  Pallas kernels: 0 us -> 145 us
  matrix products: 77.2 us -> 0 us
  other arithmetic: 59.5 us -> 0 us
  local copies, waits for them, and re-layouts: 20.5 us -> 5.05 us
  starting transfers between devices: 11.1 us -> 0 us
    psum x5 -> x0, blocking collectives: 399 us -> none  [the longest x2 172 us: projected(): return lax.psum(jnp.stack(values) / cells, ('seg', 'rad'))]
    pallas_call x0 -> x2, Pallas kernels: none -> 145 us  [the longest x1 138 us: on_device(): pl.pallas_call(functools.partial(steps_kernel, (segs, rads, group), cells...]
    dot_general x7 -> x0, matrix products: 77.2 us -> none  [the longest x2 27.2 us: tangent(): jnp.einsum('crtz,kz->crtk', mixed, anal_k, preferred_element_type=jnp.flo...]
    reduce_sum x6 -> x0, other arithmetic: 29.1 us -> none  [the longest x1 7.5 us: on_device(): jnp.sum(residual_two * residual_two)]
    convert_element_type x5 -> x0, other arithmetic: 16.1 us -> none  [the longest x2 9.19 us: tangent(): rounded = field.astype(jnp.bfloat16)]
    ppermute x6 -> x0, starting transfers between devices: 11.1 us -> none  [the longest x2 6.29 us: with_halo(): lax.ppermute(lax.slice_in_dim(block, block.shape[dim] - width, None, axis...]
    mul x2 -> x0, local copies, waits for them, and re-layouts: 10.3 us -> none  [tangent(): couple.astype(jnp.float32) * physical[None]]
  transfers between devices with their start and end apart: 6 -> 0, of which waited for: 0 -> 0; matrix products, arithmetic and copies ran while one was open for 17% -> 0% of each run, Pallas kernels for 0% -> 0%
where the time goes in v1:
time: 152 us; the launch traced here: 151 us
  Pallas kernels  145 us (95%)
  local copies, waits for them, and re-layouts  5.05 us (3%)
    pallas_call x1, Pallas kernels, on_device(): pl.pallas_call(functools.partial(steps_kernel, (segs, rads, group), cells...  138 us
    pallas_call x1, Pallas kernels, on_device(): pl.pallas_call(combine_kernel, grid=(chans, 2), out_shape=(jax.ShapeDtype...  7.51 us
    unnamed x10, local copies, waits for them, and re-layouts  5.05 us

profile of v1, /device:TPU:1, one launch (start us, length us, event | category | flops | bytes accessed | tf_op | source)
XLA Modules:
  0.0 151.5 jit_solution(960897541234981360)
XLA Ops:
  1.3 0.0 copy-start
  1.3 1.3 copy-done
  2.6 0.0 copy-start.1
  2.6 1.3 copy-done.1
  3.8 0.0 copy-start.2
  3.8 1.0 copy-done.2
  4.8 0.0 copy-start.3
  4.8 1.0 copy-done.3
  5.7 137.6 %shard_map.86 = (f32[3,384,768]{2,1,0:T(8,128)}, f32[3,384,768]{2,1,0:T(8,128)}, f32[16,128]{1,0:T(8,128)S(1)}) custom-call(f32[3,384,768]{2,1,0:T(8,128)} %bitcast.5, bf16[3,3,384,768]{3,2,1,0:T(8,128)(2,1)} %bitcast.7, f32[1]{0:T(128)S(6)} %copy.10.advect_ref, bf16[768,768]{1,0:T(8,128)(2,1)S(1)} %copy-done.1, bf16[768,768]{1,0:T(8,128)(2,1)S(1)} %copy-done, ...), custom_call_target="tpu_custom_call" | custom-call | tf_op jit(solution)/shard_map/pallas_call | solution.py:371
  143.3 0.0 copy-start.4
  143.3 0.6 copy-done.4
  143.9 7.5 %shard_map.87 = (f32[3,384,768]{2,1,0:T(8,128)}, f32[6]{0:T(128)}) custom-call(f32[16,128]{1,0:T(8,128)} %copy-done.4, f32[3,384,768]{2,1,0:T(8,128)} %bitcast.6, f32[3,384,768]{2,1,0:T(8,128)} %get-tuple-element.8.w1_ref, f32[3,384,768]{2,1,0:T(8,128)} %get-tuple-element.9.w2_ref), custom_call_target="tpu_custom_call" | custom-call | tf_op jit(solution)/shard_map/pallas_call | solution.py:411
Async XLA Ops:
  1.3 1.3 copy-start
  2.6 1.3 copy-start.1
  3.8 1.0 copy-start.2
  4.8 1.0 copy-start.3
  143.3 0.6 copy-start.4

commit v2 on v1

--- a/solution.py
+++ b/solution.py
@@ -21,6 +21,9 @@
 PARTS = 2
 STRIP = 16
 TILE = 256
+LINE = 4
+OUT_ROWS = 96
+VMEM_LIMIT = 34 * 1024 * 1024
 
 
 def make_tables(count):
@@ -51,12 +54,12 @@
 def steps_kernel(
     sizes, cells,
     v_hbm, couple_hbm, advect_ref, synth_k_hbm, anal_k_hbm, synth_m_hbm, anal_m_hbm,
-    w1_hbm, w2_hbm, coef_ref,
-    v_buf, couple, synth_k, anal_k, synth_m, anal_m,
+    v_buf, w1_buf, spec, coef_ref,
+    couple, synth_k, anal_k, synth_m, anal_m,
     sent_a, sent_b, low_a, high_a, next_a, low_b, high_b, next_b,
-    w1_buf, spec, mixed, inv_div, grams, slots_one, slots_two,
-    load_sem, v_sem, out_sem,
-    send_sem, recv_sem, sum_send, sum_recv,
+    relay_a, relay_b, mixed, inv_div, grams, slots_one, slots_two,
+    load_sem, v_sem,
+    send_sem, recv_sem, hop_send, hop_recv, sum_send, sum_recv,
 ):
     segs, rads, group = sizes
     chans, modes_m, modes_k = v_buf.shape
@@ -78,6 +81,18 @@
     def two_peer(d):
         other = lax.rem(two_me + d, two_count)
         return other, ((other // rads) * group + one_me, lax.rem(other, rads))
+
+    upper_half = seg // group
+    column, line = rad // LINE, lax.rem(rad, LINE)
+    at_edge = ((upper_half == 0) & (line == 0)) | ((upper_half == 1) & (line == LINE - 1))
+    at_far = ((upper_half == 1) & (line == 0)) | ((upper_half == 0) & (line == LINE - 1))
+    is_source = (one_me == 0) & at_edge
+    is_sink = (one_me == group - 1) & at_far
+    is_relay = (one_me == 1) & ((line == 0) | (line == LINE - 1)) & (upper_half == column)
+    relay = ((1 - column) * group + 1, (1 - column) * LINE + line)
+    relayed_rad = (1 - column) * LINE + line
+    relayed_source = (jnp.where(line == 0, 0, group), relayed_rad)
+    relayed_sink = (jnp.where(line == 0, segs - 1, group - 1), relayed_rad)
 
     loads = [
         pltpu.make_async_copy(source, target, load_sem.at[i])
@@ -107,6 +122,18 @@
     for other in (seg_prev, seg_next):
         pl.semaphore_signal(barrier, inc=1, device_id=(other, rad), device_id_type=MESH)
 
+    def signal(device):
+        pl.semaphore_signal(barrier, inc=1, device_id=device, device_id_type=MESH)
+
+    @pl.when(is_source | is_sink)
+    def _():
+        signal(relay)
+
+    @pl.when(is_relay)
+    def _():
+        signal(relayed_source)
+        signal(relayed_sink)
+
     @pl.when(rad == 0)
     def _():
         low_a[...] = jnp.zeros_like(low_a)
@@ -136,6 +163,31 @@
             copy(2, nxt, (seg_prev, rad)),
         )
 
+    def hop(phase, i):
+        c, q = pieces[i]
+        at = (c, pl.ds(q * rows, rows))
+        return pltpu.make_async_remote_copy(
+            src_ref=(sent_a, sent_b)[phase].at[at], dst_ref=(relay_a, relay_b)[phase].at[at],
+            send_sem=hop_send.at[phase, 0, i], recv_sem=hop_recv.at[phase, i],
+            device_id=relay, device_id_type=MESH,
+        )
+
+    def onward(phase, i):
+        c, q = pieces[i]
+        at = (c, pl.ds(q * rows, rows))
+        return pltpu.make_async_remote_copy(
+            src_ref=(relay_a, relay_b)[phase].at[at], dst_ref=(next_a, next_b)[phase].at[at],
+            send_sem=hop_send.at[phase, 1, i], recv_sem=recv_sem.at[phase, 2, i],
+            device_id=relayed_sink, device_id_type=MESH,
+        )
+
+    def pass_on(phase, i):
+        @pl.when(is_relay)
+        def _():
+            for j in ([0] if i == 0 else []) + ([i + 1] if i + 1 < len(pieces) else []):
+                hop(phase, j).wait_recv()
+                onward(phase, j).start()
+
     def start_sends(phase, i):
         up, down, back = sends(phase, i)
 
@@ -147,7 +199,13 @@
         def _():
             down.start()
 
-        back.start()
+        @pl.when(is_source)
+        def _():
+            hop(phase, i).start()
+
+        @pl.when(jnp.logical_not(is_source))
+        def _():
+            back.start()
 
     def wait_recvs(phase, i):
         up, down, back = sends(phase, i)
@@ -173,7 +231,17 @@
         def _():
             down.wait_send()
 
-        back.wait_send()
+        @pl.when(is_source)
+        def _():
+            hop(phase, i).wait_send()
+
+        @pl.when(jnp.logical_not(is_source))
+        def _():
+            back.wait_send()
+
+        @pl.when(is_relay)
+        def _():
+            onward(phase, i).wait_send()
 
     def strips(c, q, body, carry):
         def step(j, carry):
@@ -194,7 +262,8 @@
 
         gram[0] = strips(c, q, rounding, gram[0])
         if i == 0:
-            pl.semaphore_wait(barrier, group - 1 + two_count - 1 + 2)
+            extra = jnp.where(is_relay, 2, jnp.where(is_source | is_sink, 1, 0))
+            pl.semaphore_wait(barrier, group - 1 + two_count - 1 + 2 + extra)
         start_sends(0, i)
 
     def freq(index, count):
@@ -202,11 +271,9 @@
 
     freq_k = freq(lax.broadcasted_iota(jnp.int32, (1, modes_k), 1), modes_k)
     axial = VISC_AXIAL * (freq_k / (modes_k // 2)) ** 2
-    wavenum = freq(lax.broadcasted_iota(jnp.int32, (1, modes_k), 1), modes_k)
-    column = lax.broadcasted_iota(jnp.int32, (1, modes_k), 1)
+    mode = lax.broadcasted_iota(jnp.int32, (1, modes_k), 1)
     half = modes_k // 2
-    wavenum = jnp.where(column < half, column, half - column).astype(F32)
-    wavenum = wavenum * advect_ref[0]
+    wavenum = jnp.where(mode < half, mode, half - mode).astype(F32) * advect_ref[0]
     radius = (jnp.full((1, modes_k), rad + WINDOW_START, jnp.int32).astype(F32) + 0.5) / RADIAL_ALL
 
     def divide(j, _):
@@ -255,8 +322,8 @@
         load.wait()
     spectral(sent_a)
 
-    w1_outs = []
     for i, (c, q) in enumerate(pieces):
+        pass_on(0, i)
         wait_recvs(0, i)
 
         def first(row, at, totals, c=c):
@@ -268,14 +335,11 @@
 
         gram[1], gram[2] = strips(c, q, first, (gram[1], gram[2]))
         start_sends(1, i)
-        at = (c, pl.ds(q * rows, rows))
-        w1_outs.append(pltpu.make_async_copy(w1_buf.at[at], w1_hbm.at[at], out_sem.at[0, i]))
-        w1_outs[-1].start()
 
     spectral(sent_b)
 
-    w2_outs = []
     for i, (c, q) in enumerate(pieces):
+        pass_on(1, i)
         wait_recvs(1, i)
 
         def second(row, at, totals, c=c):
@@ -289,9 +353,6 @@
             )
 
         gram[3], gram[4], gram[5] = strips(c, q, second, (gram[3], gram[4], gram[5]))
-        at = (c, pl.ds(q * rows, rows))
-        w2_outs.append(pltpu.make_async_copy(spec.at[at], w2_hbm.at[at], out_sem.at[1, i]))
-        w2_outs[-1].start()
 
     mine = jnp.concatenate([jnp.sum(value, axis=0, keepdims=True) for value in gram] + [zero[:2]], axis=0)
 
@@ -339,20 +400,39 @@
     for i in range(len(pieces)):
         wait_sends(0, i)
         wait_sends(1, i)
-        w1_outs[i].wait()
-        w2_outs[i].wait()
-
-
-def combine_kernel(coef_ref, v_ref, w1_ref, w2_ref, out_ref, hess_ref):
-    on_two = coef_ref[6:7, 0:1]
-    on_one = coef_ref[7:8, 0:1]
-    on_start = coef_ref[8:9, 0:1]
-    out_ref[0] = on_two * w2_ref[0] + on_one * w1_ref[0] + on_start * v_ref[0]
-
-    @pl.when(pl.program_id(0) == 0)
-    def _():
-        for i in range(6):
-            hess_ref[i] = coef_ref[i, 0]
+
+
+def combine_kernel(coef_ref, v_ref, w1_ref, w2_ref, out_ref, hess_ref, stage, sem):
+    chans, modes_m, modes_k = v_ref.shape
+    on_two = jnp.broadcast_to(coef_ref[6:7, 0:1], (8, modes_k))
+    on_one = jnp.broadcast_to(coef_ref[7:8, 0:1], (8, modes_k))
+    on_start = jnp.broadcast_to(coef_ref[8:9, 0:1], (8, modes_k))
+    pieces = [(c, row) for c in range(chans) for row in range(0, modes_m, OUT_ROWS)]
+
+    def copy(i):
+        c, row = pieces[i]
+        return pltpu.make_async_copy(
+            stage.at[i % 2], out_ref.at[c, pl.ds(row, OUT_ROWS)], sem.at[i % 2]
+        )
+
+    for i, (c, row) in enumerate(pieces):
+        if i >= 2:
+            copy(i - 2).wait()
+
+        def strip(j, _, i=i, c=c, row=row):
+            at = pl.ds(pl.multiple_of(row + j * 8, 8), 8)
+            to = pl.ds(pl.multiple_of(j * 8, 8), 8)
+            stage[i % 2, to, :] = (
+                on_two * w2_ref[c, at, :] + on_one * w1_ref[c, at, :] + on_start * v_ref[c, at, :]
+            )
+            return 0
+
+        lax.fori_loop(0, OUT_ROWS // 8, strip, 0)
+        copy(i).start()
+    for i in range(6):
+        hess_ref[i] = coef_ref[i, 0]
+    copy(len(pieces) - 2).wait()
+    copy(len(pieces) - 1).wait()
 
 
 def on_device(segs, rads, start_vector, coupling, advect):
@@ -367,54 +447,52 @@
     two_count = (segs // group) * rads
     field = (chans, modes_m, modes_k)
     count = chans * PARTS
-    any_space = pl.BlockSpec(memory_space=pl.ANY)
-    w1, w2, coef = pl.pallas_call(
+    in_place = lambda value: pltpu.with_memory_space_constraint(value, pltpu.HBM)
+    tables = (synth_k, anal_k.T, synth_m.T, anal_m)
+    in_hbm = pl.BlockSpec(memory_space=pltpu.HBM)
+    in_vmem = pl.BlockSpec(memory_space=pltpu.VMEM)
+    v, w1, w2, coef = pl.pallas_call(
         functools.partial(steps_kernel, (segs, rads, group), cells),
-        out_shape=(
-            jax.ShapeDtypeStruct(field, F32),
-            jax.ShapeDtypeStruct(field, F32),
-            jax.ShapeDtypeStruct((16, 128), F32),
-        ),
-        in_specs=[any_space, any_space, pl.BlockSpec(memory_space=pltpu.SMEM)] + [any_space] * 4,
-        out_specs=(any_space, any_space, pl.BlockSpec(memory_space=pltpu.VMEM)),
+        out_shape=[jax.ShapeDtypeStruct(field, F32)] * 3 + [jax.ShapeDtypeStruct((16, 128), F32)],
+        in_specs=[in_hbm, in_hbm, pl.BlockSpec(memory_space=pltpu.SMEM)] + [in_hbm] * 4,
+        out_specs=[in_vmem] * 4,
         scratch_shapes=[
-            pltpu.VMEM(field, F32),
             pltpu.VMEM((chans,) + field, BF16),
             pltpu.VMEM((modes_k, modes_k), BF16),
             pltpu.VMEM((modes_k, modes_k), BF16),
             pltpu.VMEM((modes_m, modes_m), BF16),
             pltpu.VMEM((modes_m, modes_m), BF16),
         ]
-        + [pltpu.VMEM(field, BF16)] * 8
+        + [pltpu.VMEM(field, BF16)] * 11
         + [
-            pltpu.VMEM(field, F32),
-            pltpu.VMEM(field, F32),
-            pltpu.VMEM(field, BF16),
             pltpu.VMEM((modes_m, modes_k), F32),
             pltpu.VMEM((8, 128), F32),
             pltpu.VMEM((group, 8, 128), F32),
             pltpu.VMEM((two_count, 8, 128), F32),
             pltpu.SemaphoreType.DMA((5,)),
             pltpu.SemaphoreType.DMA((count,)),
-            pltpu.SemaphoreType.DMA((2, count)),
             pltpu.SemaphoreType.DMA((2, 3, count)),
             pltpu.SemaphoreType.DMA((2, 3, count)),
+            pltpu.SemaphoreType.DMA((2, 2, count)),
+            pltpu.SemaphoreType.DMA((2, count)),
             pltpu.SemaphoreType.DMA((2, 16)),
             pltpu.SemaphoreType.DMA((2, 16)),
         ],
         compiler_params=pltpu.CompilerParams(
-            collective_id=0, has_side_effects=True, vmem_limit_bytes=50 * 1024 * 1024
+            collective_id=0, has_side_effects=True, vmem_limit_bytes=VMEM_LIMIT
         ),
-    )(vector, couple, advect, synth_k, anal_k.T, synth_m.T, anal_m)
-    block = (1, modes_m // 2, modes_k)
-    block_spec = pl.BlockSpec(block, lambda c, q: (c, q, 0))
+    )(in_place(vector), in_place(couple), advect, *map(in_place, tables))
     out, hess = pl.pallas_call(
         combine_kernel,
-        grid=(chans, 2),
         out_shape=(jax.ShapeDtypeStruct(field, F32), jax.ShapeDtypeStruct((6,), F32)),
-        in_specs=[pl.BlockSpec((16, 128), lambda c, q: (0, 0))] + [block_spec] * 3,
-        out_specs=(block_spec, pl.BlockSpec(memory_space=pltpu.SMEM)),
-    )(coef, vector, w1, w2)
+        in_specs=[in_vmem] * 4,
+        out_specs=(in_hbm, pl.BlockSpec(memory_space=pltpu.SMEM)),
+        scratch_shapes=[
+            pltpu.VMEM((2, OUT_ROWS, modes_k), F32),
+            pltpu.SemaphoreType.DMA((2,)),
+        ],
+        compiler_params=pltpu.CompilerParams(vmem_limit_bytes=VMEM_LIMIT),
+    )(coef, v, w1, w2)
     return out.reshape(shape), hess
 
 

time: 152 us -> 183 us (1.20)
  Pallas kernels: 145 us -> 181 us
  local copies, waits for them, and re-layouts: 5.05 us -> 0 us
    pallas_call x1, Pallas kernels: 138 us -> 176 us  [on_device(): pl.pallas_call(functools.partial(steps_kernel, (segs, rads, group), cells...]
    unnamed x10 -> x0, local copies, waits for them, and re-layouts: 5.05 us -> none
where the time goes in v2:
time: 183 us
  Pallas kernels  181 us (99%)
    pallas_call x1, Pallas kernels, on_device(): pl.pallas_call(functools.partial(steps_kernel, (segs, rads, group), cells...  176 us
    pallas_call x1, Pallas kernels, on_device(): pl.pallas_call(combine_kernel, out_shape=(jax.ShapeDtypeStruct(field, F32...  5.7 us

profile of v2, /device:TPU:1, one launch (start us, length us, event | category | flops | bytes accessed | tf_op | source)
XLA Modules:
  0.0 182.6 jit_solution(3724327964146404221)
XLA Ops:
  1.3 175.6 %shard_map.86 = (f32[3,384,768]{2,1,0:T(8,128)S(1)}, f32[3,384,768]{2,1,0:T(8,128)S(1)}, f32[3,384,768]{2,1,0:T(8,128)S(1)}, f32[16,128]{1,0:T(8,128)S(1)}) custom-call(f32[3,384,768]{2,1,0:T(8,128)} %bitcast.6, bf16[3,3,384,768]{3,2,1,0:T(8,128)(2,1)} %bitcast.5, f32[1]{0:T(128)S(6)} %copy.10.advect_ref, bf16[768,768]{1,0:T(8,128)(2,1)} %constant.10.clone.synth_k_hbm, ...), custom_call_target="tpu_custom_call" | custom-call | tf_op jit(solution)/shard_map/pallas_call | solution.py:454
  176.9 5.7 %shard_map.87 = (f32[3,384,768]{2,1,0:T(8,128)}, f32[6]{0:T(128)}) custom-call(f32[16,128]{1,0:T(8,128)S(1)} %get-tuple-element.8.coef_ref, f32[3,384,768]{2,1,0:T(8,128)S(1)} %get-tuple-element.9.v_ref, f32[3,384,768]{2,1,0:T(8,128)S(1)} %get-tuple-element.10.w1_ref, f32[3,384,768]{2,1,0:T(8,128)S(1)} %get-tuple-element.11.w2_ref), custom_call_target="tpu_custom_call" | custom-call | tf_op jit(solution)/shard_map/pallas_call | solution.py:485

commit v3 on v2

--- a/solution.py
+++ b/solution.py
@@ -23,6 +23,7 @@
 TILE = 256
 LINE = 4
 OUT_ROWS = 96
+OUT_STRIP = 32
 VMEM_LIMIT = 34 * 1024 * 1024
 
 
@@ -84,15 +85,14 @@
 
     upper_half = seg // group
     column, line = rad // LINE, lax.rem(rad, LINE)
-    at_edge = ((upper_half == 0) & (line == 0)) | ((upper_half == 1) & (line == LINE - 1))
-    at_far = ((upper_half == 1) & (line == 0)) | ((upper_half == 0) & (line == LINE - 1))
-    is_source = (one_me == 0) & at_edge
-    is_sink = (one_me == group - 1) & at_far
-    is_relay = (one_me == 1) & ((line == 0) | (line == LINE - 1)) & (upper_half == column)
-    relay = ((1 - column) * group + 1, (1 - column) * LINE + line)
-    relayed_rad = (1 - column) * LINE + line
-    relayed_source = (jnp.where(line == 0, 0, group), relayed_rad)
-    relayed_sink = (jnp.where(line == 0, segs - 1, group - 1), relayed_rad)
+    far_rad = (1 - column) * LINE + line
+    detoured = ((line == LINE - 1) & (column == 0)) | ((line == 0) & (column == 1))
+    is_source = (one_me == 0) & detoured
+    is_sink = (one_me == group - 1) & detoured
+    is_relay = (one_me == 1) & (((line == LINE - 1) & (column == 1)) | ((line == 0) & (column == 0)))
+    relay = ((1 - upper_half) * group + 1, far_rad)
+    relayed_source = ((1 - upper_half) * group, far_rad)
+    relayed_sink = (base + group - 1, far_rad)
 
     loads = [
         pltpu.make_async_copy(source, target, load_sem.at[i])
@@ -125,24 +125,18 @@
     def signal(device):
         pl.semaphore_signal(barrier, inc=1, device_id=device, device_id_type=MESH)
 
-    @pl.when(is_source | is_sink)
+    @pl.when(is_source)
     def _():
         signal(relay)
+
+    @pl.when(is_sink)
+    def _():
+        signal((base + 1, far_rad))
 
     @pl.when(is_relay)
     def _():
         signal(relayed_source)
         signal(relayed_sink)
-
-    @pl.when(rad == 0)
-    def _():
-        low_a[...] = jnp.zeros_like(low_a)
-        low_b[...] = jnp.zeros_like(low_b)
-
-    @pl.when(rad == rads - 1)
-    def _():
-        high_a[...] = jnp.zeros_like(high_a)
-        high_b[...] = jnp.zeros_like(high_b)
 
     def sends(phase, i):
         c, q = pieces[i]
@@ -265,6 +259,16 @@
             extra = jnp.where(is_relay, 2, jnp.where(is_source | is_sink, 1, 0))
             pl.semaphore_wait(barrier, group - 1 + two_count - 1 + 2 + extra)
         start_sends(0, i)
+
+    @pl.when(rad == 0)
+    def _():
+        low_a[...] = jnp.zeros_like(low_a)
+        low_b[...] = jnp.zeros_like(low_b)
+
+    @pl.when(rad == rads - 1)
+    def _():
+        high_a[...] = jnp.zeros_like(high_a)
+        high_b[...] = jnp.zeros_like(high_b)
 
     def freq(index, count):
         return jnp.where(index <= count // 2, index, index - count // 2).astype(F32)
@@ -404,35 +408,31 @@
 
 def combine_kernel(coef_ref, v_ref, w1_ref, w2_ref, out_ref, hess_ref, stage, sem):
     chans, modes_m, modes_k = v_ref.shape
-    on_two = jnp.broadcast_to(coef_ref[6:7, 0:1], (8, modes_k))
-    on_one = jnp.broadcast_to(coef_ref[7:8, 0:1], (8, modes_k))
-    on_start = jnp.broadcast_to(coef_ref[8:9, 0:1], (8, modes_k))
+    on_two = jnp.broadcast_to(coef_ref[6:7, 0:1], (OUT_STRIP, modes_k))
+    on_one = jnp.broadcast_to(coef_ref[7:8, 0:1], (OUT_STRIP, modes_k))
+    on_start = jnp.broadcast_to(coef_ref[8:9, 0:1], (OUT_STRIP, modes_k))
     pieces = [(c, row) for c in range(chans) for row in range(0, modes_m, OUT_ROWS)]
 
     def copy(i):
         c, row = pieces[i]
-        return pltpu.make_async_copy(
-            stage.at[i % 2], out_ref.at[c, pl.ds(row, OUT_ROWS)], sem.at[i % 2]
-        )
+        at = (c, pl.ds(row, OUT_ROWS))
+        return pltpu.make_async_copy(stage.at[at], out_ref.at[at], sem.at[i])
 
     for i, (c, row) in enumerate(pieces):
-        if i >= 2:
-            copy(i - 2).wait()
-
-        def strip(j, _, i=i, c=c, row=row):
-            at = pl.ds(pl.multiple_of(row + j * 8, 8), 8)
-            to = pl.ds(pl.multiple_of(j * 8, 8), 8)
-            stage[i % 2, to, :] = (
+
+        def strip(j, _, c=c, row=row):
+            at = pl.ds(pl.multiple_of(row + j * OUT_STRIP, OUT_STRIP), OUT_STRIP)
+            stage[c, at, :] = (
                 on_two * w2_ref[c, at, :] + on_one * w1_ref[c, at, :] + on_start * v_ref[c, at, :]
             )
             return 0
 
-        lax.fori_loop(0, OUT_ROWS // 8, strip, 0)
+        lax.fori_loop(0, OUT_ROWS // OUT_STRIP, strip, 0)
         copy(i).start()
     for i in range(6):
         hess_ref[i] = coef_ref[i, 0]
-    copy(len(pieces) - 2).wait()
-    copy(len(pieces) - 1).wait()
+    for i in range(len(pieces)):
+        copy(i).wait()
 
 
 def on_device(segs, rads, start_vector, coupling, advect):
@@ -488,8 +488,8 @@
         in_specs=[in_vmem] * 4,
         out_specs=(in_hbm, pl.BlockSpec(memory_space=pltpu.SMEM)),
         scratch_shapes=[
-            pltpu.VMEM((2, OUT_ROWS, modes_k), F32),
-            pltpu.SemaphoreType.DMA((2,)),
+            pltpu.VMEM(field, F32),
+            pltpu.SemaphoreType.DMA((chans * modes_m // OUT_ROWS,)),
         ],
         compiler_params=pltpu.CompilerParams(vmem_limit_bytes=VMEM_LIMIT),
     )(coef, v, w1, w2)

time: 183 us -> 105 us (0.57)
  Pallas kernels: 181 us -> 103 us
    pallas_call x1, Pallas kernels: 176 us -> 101 us  [on_device(): pl.pallas_call(functools.partial(steps_kernel, (segs, rads, group), cells...]
    pallas_call x1, Pallas kernels: 5.7 us -> 2.51 us  [on_device(): pl.pallas_call(combine_kernel, out_shape=(jax.ShapeDtypeStruct(field, F32...]
where the time goes in v3:
time: 105 us; the launch traced here: 104 us
  Pallas kernels  103 us (98%)
  between operations  1.28 us (1%)
    pallas_call x1, Pallas kernels, on_device(): pl.pallas_call(functools.partial(steps_kernel, (segs, rads, group), cells...  101 us
    pallas_call x1, Pallas kernels, on_device(): pl.pallas_call(combine_kernel, out_shape=(jax.ShapeDtypeStruct(field, F32...  2.51 us

profile of v3, /device:TPU:1, one launch (start us, length us, event | category | flops | bytes accessed | tf_op | source)
XLA Modules:
  0.0 104.5 jit_solution(6498366837161160468)
XLA Ops:
  1.3 100.7 %shard_map.86 = (f32[3,384,768]{2,1,0:T(8,128)S(1)}, f32[3,384,768]{2,1,0:T(8,128)S(1)}, f32[3,384,768]{2,1,0:T(8,128)S(1)}, f32[16,128]{1,0:T(8,128)S(1)}) custom-call(f32[3,384,768]{2,1,0:T(8,128)} %bitcast.6, bf16[3,3,384,768]{3,2,1,0:T(8,128)(2,1)} %bitcast.5, f32[1]{0:T(128)S(6)} %copy.10.advect_ref, bf16[768,768]{1,0:T(8,128)(2,1)} %constant.10.clone.synth_k_hbm, ...), custom_call_target="tpu_custom_call" | custom-call | tf_op jit(solution)/shard_map/pallas_call | solution.py:454
  102.0 2.5 %shard_map.87 = (f32[3,384,768]{2,1,0:T(8,128)}, f32[6]{0:T(128)}) custom-call(f32[16,128]{1,0:T(8,128)S(1)} %get-tuple-element.8.coef_ref, f32[3,384,768]{2,1,0:T(8,128)S(1)} %get-tuple-element.9.v_ref, f32[3,384,768]{2,1,0:T(8,128)S(1)} %get-tuple-element.10.w1_ref, f32[3,384,768]{2,1,0:T(8,128)S(1)} %get-tuple-element.11.w2_ref), custom_call_target="tpu_custom_call" | custom-call | tf_op jit(solution)/shard_map/pallas_call | solution.py:485

commit v4 on v3

--- a/solution.py
+++ b/solution.py
@@ -22,6 +22,11 @@
 STRIP = 16
 TILE = 256
 LINE = 4
+REACH = (1, 2, 4)
+FAR_FIRST = (
+    (8, 7, 9, 6, 10, 5, 11, 4, 12, 3, 13, 2, 14, 1, 15),
+    (10, 6, 9, 7, 8, 11, 5, 2, 14, 3, 13, 12, 4, 1, 15),
+)
 OUT_ROWS = 96
 OUT_STRIP = 32
 VMEM_LIMIT = 34 * 1024 * 1024
@@ -58,9 +63,9 @@
     v_buf, w1_buf, spec, coef_ref,
     couple, synth_k, anal_k, synth_m, anal_m,
     sent_a, sent_b, low_a, high_a, next_a, low_b, high_b, next_b,
-    relay_a, relay_b, mixed, inv_div, grams, slots_one, slots_two,
+    relay_a, relay_b, mixed, inv_div, slots_one, slots_two,
     load_sem, v_sem,
-    send_sem, recv_sem, hop_send, hop_recv, sum_send, sum_recv,
+    send_sem, recv_sem, hop_send, hop_recv, sum_send, sum_recv, met_sem,
 ):
     segs, rads, group = sizes
     chans, modes_m, modes_k = v_buf.shape
@@ -111,19 +116,22 @@
         at = (c, pl.ds(q * rows, rows))
         v_loads.append(pltpu.make_async_copy(v_hbm.at[at], v_buf.at[at], v_sem.at[i]))
         v_loads[-1].start()
-    for load in loads:
-        load.start()
 
     barrier = pltpu.get_barrier_semaphore()
-    for d in range(1, group):
-        pl.semaphore_signal(barrier, inc=1, device_id=(base + one_peer(d), rad), device_id_type=MESH)
-    for d in range(1, two_count):
-        pl.semaphore_signal(barrier, inc=1, device_id=two_peer(d)[1], device_id_type=MESH)
-    for other in (seg_prev, seg_next):
-        pl.semaphore_signal(barrier, inc=1, device_id=(other, rad), device_id_type=MESH)
+
+    def ring(which, offset):
+        if which == 0:
+            return base + lax.rem(one_me + group + offset, group), rad
+        return two_peer(two_count + offset)[1]
 
     def signal(device):
         pl.semaphore_signal(barrier, inc=1, device_id=device, device_id_type=MESH)
+
+    for other in (seg_prev, seg_next):
+        signal((other, rad))
+    for which in range(2):
+        signal(ring(which, 1))
+        signal(ring(which, -1))
 
     @pl.when(is_source)
     def _():
@@ -137,6 +145,18 @@
     def _():
         signal(relayed_source)
         signal(relayed_sink)
+
+    for load in loads:
+        load.start()
+
+    def say_met(step):
+        for which in range(2):
+            for offset in (REACH[step], -REACH[step]):
+                pl.semaphore_signal(met_sem.at[which, step], inc=1, device_id=ring(which, offset), device_id_type=MESH)
+
+    def wait_met(step):
+        for which in range(2):
+            pl.semaphore_wait(met_sem.at[which, step], 2)
 
     def sends(phase, i):
         c, q = pieces[i]
@@ -257,7 +277,7 @@
         gram[0] = strips(c, q, rounding, gram[0])
         if i == 0:
             extra = jnp.where(is_relay, 2, jnp.where(is_source | is_sink, 1, 0))
-            pl.semaphore_wait(barrier, group - 1 + two_count - 1 + 2 + extra)
+            pl.semaphore_wait(barrier, 6 + extra)
         start_sends(0, i)
 
     @pl.when(rad == 0)
@@ -269,6 +289,8 @@
     def _():
         high_a[...] = jnp.zeros_like(high_a)
         high_b[...] = jnp.zeros_like(high_b)
+
+    say_met(0)
 
     def freq(index, count):
         return jnp.where(index <= count // 2, index, index - count // 2).astype(F32)
@@ -325,6 +347,8 @@
     for load in loads:
         load.wait()
     spectral(sent_a)
+    wait_met(0)
+    say_met(1)
 
     for i, (c, q) in enumerate(pieces):
         pass_on(0, i)
@@ -339,11 +363,16 @@
 
         gram[1], gram[2] = strips(c, q, first, (gram[1], gram[2]))
         start_sends(1, i)
+        if i == 0:
+            wait_met(1)
+            say_met(2)
+    wait_met(2)
 
     spectral(sent_b)
 
     for i, (c, q) in enumerate(pieces):
         pass_on(1, i)
+        wait_sends(0, i)
         wait_recvs(1, i)
 
         def second(row, at, totals, c=c):
@@ -358,32 +387,50 @@
 
         gram[3], gram[4], gram[5] = strips(c, q, second, (gram[3], gram[4], gram[5]))
 
-    mine = jnp.concatenate([jnp.sum(value, axis=0, keepdims=True) for value in gram] + [zero[:2]], axis=0)
-
-    def add_up(stage, slots, me, count, peer):
-        def copy(d, slot):
-            return pltpu.make_async_remote_copy(
-                src_ref=slots.at[slot], dst_ref=slots.at[slot],
-                send_sem=sum_send.at[stage, d], recv_sem=sum_recv.at[stage, d],
-                device_id=peer(d), device_id_type=MESH,
-            )
-
-        for d in range(1, count):
-            copy(d, me).start()
-        for d in range(1, count):
-            copy(d, lax.rem(me + count - d, count)).wait_recv()
+    here = lax.broadcasted_iota(jnp.int32, (8, 128), 0) == lax.broadcasted_iota(jnp.int32, (8, 128), 1)
+    rows_of = jnp.concatenate([jnp.sum(value, axis=0, keepdims=True) for value in gram] + [zero[:2]], axis=0)
+    mine = jnp.sum(jnp.where(here, jnp.sum(rows_of, axis=1, keepdims=True), 0.0), axis=0, keepdims=True)
+    stages = (
+        (slots_one, one_me, group, lambda d: (base + one_peer(d), rad)),
+        (slots_two, two_me, two_count, lambda d: two_peer(d)[1]),
+    )
+
+    def message(stage, d, slot):
+        slots, _, _, peer = stages[stage]
+        return pltpu.make_async_remote_copy(
+            src_ref=slots.at[slot], dst_ref=slots.at[slot],
+            send_sem=sum_send.at[stage, d], recv_sem=sum_recv.at[stage, d],
+            device_id=peer(d), device_id_type=MESH,
+        )
+
+    def send_sums(stage, value):
+        slots, me, _, _ = stages[stage]
+        slots[me] = value
+        for d in FAR_FIRST[stage]:
+            message(stage, d, me).start()
+
+    def total_of(stage):
+        slots, me, count, _ = stages[stage]
+        for d in FAR_FIRST[stage][::-1]:
+            message(stage, d, lax.rem(me + count - d, count)).wait_recv()
         total = slots[0]
         for slot in range(1, count):
             total = total + slots[slot]
-        for d in range(1, count):
-            copy(d, me).wait_send()
         return total
 
-    slots_one[one_me] = mine
-    partial = add_up(0, slots_one, one_me, group, lambda d: (base + one_peer(d), rad))
-    slots_two[two_me] = partial
-    sums = add_up(1, slots_two, two_me, two_count, lambda d: two_peer(d)[1])
-    sums = jnp.broadcast_to(jnp.sum(sums, axis=1, keepdims=True), (8, 128)) * (1.0 / cells)
+    def sums_sent(stage):
+        for d in FAR_FIRST[stage]:
+            message(stage, d, stages[stage][1]).wait_send()
+
+    send_sums(0, mine)
+    for i in range(len(pieces)):
+        wait_sends(1, i)
+    partial = total_of(0)
+    send_sums(1, partial)
+    sums_sent(0)
+    sums = jnp.broadcast_to(total_of(1), (8, 128))
+    sums = jnp.sum(jnp.where(here, sums, 0.0), axis=1, keepdims=True) * (1.0 / cells)
+    sums = jnp.broadcast_to(sums, (8, 128))
     g00, g01, g11, g02, g12, g22 = (sums[i : i + 1] for i in range(6))
     start_norm = jnp.sqrt(g00)
     upper_one = g01 / g00
@@ -401,9 +448,7 @@
     )
     coef_ref[8:16, :] = jnp.broadcast_to(on_start, (8, 128))
 
-    for i in range(len(pieces)):
-        wait_sends(0, i)
-        wait_sends(1, i)
+    sums_sent(1)
 
 
 def combine_kernel(coef_ref, v_ref, w1_ref, w2_ref, out_ref, hess_ref, stage, sem):
@@ -466,9 +511,8 @@
         + [pltpu.VMEM(field, BF16)] * 11
         + [
             pltpu.VMEM((modes_m, modes_k), F32),
-            pltpu.VMEM((8, 128), F32),
-            pltpu.VMEM((group, 8, 128), F32),
-            pltpu.VMEM((two_count, 8, 128), F32),
+            pltpu.VMEM((group, 1, 128), F32),
+            pltpu.VMEM((two_count, 1, 128), F32),
             pltpu.SemaphoreType.DMA((5,)),
             pltpu.SemaphoreType.DMA((count,)),
             pltpu.SemaphoreType.DMA((2, 3, count)),
@@ -477,6 +521,7 @@
             pltpu.SemaphoreType.DMA((2, count)),
             pltpu.SemaphoreType.DMA((2, 16)),
             pltpu.SemaphoreType.DMA((2, 16)),
+            pltpu.SemaphoreType.REGULAR((2, len(REACH))),
         ],
         compiler_params=pltpu.CompilerParams(
             collective_id=0, has_side_effects=True, vmem_limit_bytes=VMEM_LIMIT

time: 105 us -> 103 us (0.981)
  Pallas kernels: 103 us -> 101 us
    pallas_call x1, Pallas kernels: 101 us -> 98.8 us  [on_device(): pl.pallas_call(functools.partial(steps_kernel, (segs, rads, group), cells...]
where the time goes in v4:
time: 103 us
  Pallas kernels  101 us (98%)
  between operations  1.28 us (1%)
    pallas_call x1, Pallas kernels, on_device(): pl.pallas_call(functools.partial(steps_kernel, (segs, rads, group), cells...  98.8 us
    pallas_call x1, Pallas kernels, on_device(): pl.pallas_call(combine_kernel, out_shape=(jax.ShapeDtypeStruct(field, F32...  2.51 us

profile of v4, /device:TPU:1, one launch (start us, length us, event | category | flops | bytes accessed | tf_op | source)
XLA Modules:
  0.0 102.6 jit_solution(3556201877762013274)
XLA Ops:
  1.3 98.8 %shard_map.86 = (f32[3,384,768]{2,1,0:T(8,128)S(1)}, f32[3,384,768]{2,1,0:T(8,128)S(1)}, f32[3,384,768]{2,1,0:T(8,128)S(1)}, f32[16,128]{1,0:T(8,128)S(1)}) custom-call(f32[3,384,768]{2,1,0:T(8,128)} %bitcast.6, bf16[3,3,384,768]{3,2,1,0:T(8,128)(2,1)} %bitcast.5, f32[1]{0:T(128)S(6)} %copy.10.advect_ref, bf16[768,768]{1,0:T(8,128)(2,1)} %constant.10.clone.synth_k_hbm, ...), custom_call_target="tpu_custom_call" | custom-call | tf_op jit(solution)/shard_map/pallas_call | solution.py:499
  100.1 2.5 %shard_map.87 = (f32[3,384,768]{2,1,0:T(8,128)}, f32[6]{0:T(128)}) custom-call(f32[16,128]{1,0:T(8,128)S(1)} %get-tuple-element.8.coef_ref, f32[3,384,768]{2,1,0:T(8,128)S(1)} %get-tuple-element.9.v_ref, f32[3,384,768]{2,1,0:T(8,128)S(1)} %get-tuple-element.10.w1_ref, f32[3,384,768]{2,1,0:T(8,128)S(1)} %get-tuple-element.11.w2_ref), custom_call_target="tpu_custom_call" | custom-call | tf_op jit(solution)/shard_map/pallas_call | solution.py:530

commit v5 on v4

--- a/solution.py
+++ b/solution.py
@@ -432,17 +432,23 @@
     sums = jnp.sum(jnp.where(here, sums, 0.0), axis=1, keepdims=True) * (1.0 / cells)
     sums = jnp.broadcast_to(sums, (8, 128))
     g00, g01, g11, g02, g12, g22 = (sums[i : i + 1] for i in range(6))
+    by_start = 1.0 / g00
+    upper_one = g01 * by_start
+    rest_one = g11 - upper_one * g01
+    by_rest = 1.0 / rest_one
+    along_start = g02 - upper_one * g01
+    along_rest = g12 - upper_one * (g02 + g11) + upper_one * upper_one * g01
+    length = g22 - 2.0 * upper_one * g12 + upper_one * upper_one * g11
+    middle_two = along_rest * by_rest
+    start_part = along_start * by_start
+    rest_two = length - along_start * start_part - along_rest * middle_two
+    on_two = 1.0 / jnp.sqrt(rest_two)
+    on_one = -(upper_one + middle_two) * on_two
+    on_start = (upper_one * middle_two - start_part) * on_two
     start_norm = jnp.sqrt(g00)
-    upper_one = g01 / g00
-    lower_one = jnp.sqrt(g11 / g00 - upper_one * upper_one)
-    scale = start_norm * lower_one
-    upper_two = (g02 - upper_one * g01) / (g00 * lower_one)
-    middle_two = (g12 - upper_one * (g02 + g11) + upper_one * upper_one * g01) / (scale * scale)
-    length = (g22 - 2.0 * upper_one * g12 + upper_one * upper_one * g11) / (scale * scale)
-    lower_two = jnp.sqrt(length - upper_two * upper_two - middle_two * middle_two)
-    on_two = 1.0 / (scale * lower_two)
-    on_one = -(upper_one + middle_two) * on_two
-    on_start = (middle_two * upper_one / scale - upper_two / start_norm) / lower_two
+    lower_one = jnp.sqrt(rest_one * by_start)
+    upper_two = start_part / lower_one
+    lower_two = jnp.sqrt(rest_two * by_rest)
     coef_ref[0:8, :] = jnp.concatenate(
         [start_norm, upper_one, lower_one, upper_two, middle_two, lower_two, on_two, on_one], axis=0
     )

time: 103 us -> 103 us (level)
  no operation moved by 1% of the time
where the time goes in v5:
time: 103 us
  Pallas kernels  101 us (98%)
  between operations  1.28 us (1%)
    pallas_call x1, Pallas kernels, on_device(): pl.pallas_call(functools.partial(steps_kernel, (segs, rads, group), cells...  98.8 us
    pallas_call x1, Pallas kernels, on_device(): pl.pallas_call(combine_kernel, out_shape=(jax.ShapeDtypeStruct(field, F32...  2.51 us

profile of v5, /device:TPU:1, one launch (start us, length us, event | category | flops | bytes accessed | tf_op | source)
XLA Modules:
  0.0 102.6 jit_solution(12474549832166746564)
XLA Ops:
  1.3 98.8 %shard_map.86 = (f32[3,384,768]{2,1,0:T(8,128)S(1)}, f32[3,384,768]{2,1,0:T(8,128)S(1)}, f32[3,384,768]{2,1,0:T(8,128)S(1)}, f32[16,128]{1,0:T(8,128)S(1)}) custom-call(f32[3,384,768]{2,1,0:T(8,128)} %bitcast.6, bf16[3,3,384,768]{3,2,1,0:T(8,128)(2,1)} %bitcast.5, f32[1]{0:T(128)S(6)} %copy.10.advect_ref, bf16[768,768]{1,0:T(8,128)(2,1)} %constant.10.clone.synth_k_hbm, ...), custom_call_target="tpu_custom_call" | custom-call | tf_op jit(solution)/shard_map/pallas_call | solution.py:505
  100.0 2.5 %shard_map.87 = (f32[3,384,768]{2,1,0:T(8,128)}, f32[6]{0:T(128)}) custom-call(f32[16,128]{1,0:T(8,128)S(1)} %get-tuple-element.8.coef_ref, f32[3,384,768]{2,1,0:T(8,128)S(1)} %get-tuple-element.9.v_ref, f32[3,384,768]{2,1,0:T(8,128)S(1)} %get-tuple-element.10.w1_ref, f32[3,384,768]{2,1,0:T(8,128)S(1)} %get-tuple-element.11.w2_ref), custom_call_target="tpu_custom_call" | custom-call | tf_op jit(solution)/shard_map/pallas_call | solution.py:536

commit v6 on v4

--- a/solution.py
+++ b/solution.py
@@ -19,7 +19,7 @@
 F32 = jnp.float32
 BF16 = jnp.bfloat16
 PARTS = 2
-STRIP = 16
+STRIP = 32
 TILE = 256
 LINE = 4
 REACH = (1, 2, 4)
@@ -99,6 +99,35 @@
     relayed_source = ((1 - upper_half) * group, far_rad)
     relayed_sink = (base + group - 1, far_rad)
 
+    barrier = pltpu.get_barrier_semaphore()
+
+    def ring(which, offset):
+        if which == 0:
+            return base + lax.rem(one_me + group + offset, group), rad
+        return two_peer(two_count + offset)[1]
+
+    def signal(device):
+        pl.semaphore_signal(barrier, inc=1, device_id=device, device_id_type=MESH)
+
+    for which in (1, 0):
+        signal(ring(which, 1))
+        signal(ring(which, -1))
+    for other in (seg_prev, seg_next):
+        signal((other, rad))
+
+    @pl.when(is_source)
+    def _():
+        signal(relay)
+
+    @pl.when(is_sink)
+    def _():
+        signal((base + 1, far_rad))
+
+    @pl.when(is_relay)
+    def _():
+        signal(relayed_source)
+        signal(relayed_sink)
+
     loads = [
         pltpu.make_async_copy(source, target, load_sem.at[i])
         for i, (source, target) in enumerate(
@@ -116,35 +145,6 @@
         at = (c, pl.ds(q * rows, rows))
         v_loads.append(pltpu.make_async_copy(v_hbm.at[at], v_buf.at[at], v_sem.at[i]))
         v_loads[-1].start()
-
-    barrier = pltpu.get_barrier_semaphore()
-
-    def ring(which, offset):
-        if which == 0:
-            return base + lax.rem(one_me + group + offset, group), rad
-        return two_peer(two_count + offset)[1]
-
-    def signal(device):
-        pl.semaphore_signal(barrier, inc=1, device_id=device, device_id_type=MESH)
-
-    for other in (seg_prev, seg_next):
-        signal((other, rad))
-    for which in range(2):
-        signal(ring(which, 1))
-        signal(ring(which, -1))
-
-    @pl.when(is_source)
-    def _():
-        signal(relay)
-
-    @pl.when(is_sink)
-    def _():
-        signal((base + 1, far_rad))
-
-    @pl.when(is_relay)
-    def _():
-        signal(relayed_source)
-        signal(relayed_sink)
 
     for load in loads:
         load.start()

time: 103 us -> 103 us (level)
  no operation moved by 1% of the time
where the time goes in v6:
time: 103 us; the launch traced here: 102 us
  Pallas kernels  101 us (98%)
  between operations  1.28 us (1%)
    pallas_call x1, Pallas kernels, on_device(): pl.pallas_call(functools.partial(steps_kernel, (segs, rads, group), cells...  98.7 us
    pallas_call x1, Pallas kernels, on_device(): pl.pallas_call(combine_kernel, out_shape=(jax.ShapeDtypeStruct(field, F32...  2.51 us

profile of v6, /device:TPU:1, one launch (start us, length us, event | category | flops | bytes accessed | tf_op | source)
XLA Modules:
  0.0 102.5 jit_solution(4562746901453866800)
XLA Ops:
  1.3 98.7 %shard_map.86 = (f32[3,384,768]{2,1,0:T(8,128)S(1)}, f32[3,384,768]{2,1,0:T(8,128)S(1)}, f32[3,384,768]{2,1,0:T(8,128)S(1)}, f32[16,128]{1,0:T(8,128)S(1)}) custom-call(f32[3,384,768]{2,1,0:T(8,128)} %bitcast.6, bf16[3,3,384,768]{3,2,1,0:T(8,128)(2,1)} %bitcast.5, f32[1]{0:T(128)S(6)} %copy.10.advect_ref, bf16[768,768]{1,0:T(8,128)(2,1)} %constant.10.clone.synth_k_hbm, ...), custom_call_target="tpu_custom_call" | custom-call | tf_op jit(solution)/shard_map/pallas_call | solution.py:499
  100.0 2.5 %shard_map.87 = (f32[3,384,768]{2,1,0:T(8,128)}, f32[6]{0:T(128)}) custom-call(f32[16,128]{1,0:T(8,128)S(1)} %get-tuple-element.8.coef_ref, f32[3,384,768]{2,1,0:T(8,128)S(1)} %get-tuple-element.9.v_ref, f32[3,384,768]{2,1,0:T(8,128)S(1)} %get-tuple-element.10.w1_ref, f32[3,384,768]{2,1,0:T(8,128)S(1)} %get-tuple-element.11.w2_ref), custom_call_target="tpu_custom_call" | custom-call | tf_op jit(solution)/shard_map/pallas_call | solution.py:530
